TPU v7x, 32 devices: a whole 2x2x4 slice. The times are simulated.
32 devices in a mesh: lon: 8 (over z, x), grp: 4 (over y, core).
Axes of the slice: x: 2, y: 2, z: 4, core: 2. Of those that a mesh axis runs over, the one named last changes fastest.
Arguments:
- ray_weights: bfloat16 [16384, 128], P(('lon', 'grp')), may hold values from 0.049804688 to 0.44921875
- ray_sector: int32 [16384, 1], P(('lon', 'grp')), may hold values from 0 to 7; in each aligned block of 512 rows (0 to 511, 512 to 1023, ...) at most 128 rows name the same one
- ray_block: int32 [16384], P(('lon', 'grp')), may hold values from 0 to 1023
- ray_offset: int32 [16384], P(('lon', 'grp')), may hold values from 0 to 384
- ray_resid: float32 [16384], P(('lon', 'grp')), may hold values from -6 to 6
- smooth_resid: float32 [16, 512, 512], P('lon'), may hold values from -6 to 6
- model_dir: float32 [16, 512, 512], P('lon'), may hold values from -6 to 6
- search_dir: float32 [16, 512, 512], P('lon'), may hold values from -6 to 6
- model: float32 [16, 512, 512], P('lon'), may hold values from -6 to 6
- stencil_coeffs: float32 [4], replicated, may hold values from 0.05 to 0.3
- lsqr_scalars: float32 [3], replicated, may hold values from 0.5 to 2
Outputs:
- model_new: float32 [16, 512, 512], P('lon')
- search_new: float32 [16, 512, 512], P('lon')
- dir_new: float32 [16, 512, 512], P('lon')
- ray_resid_new: float32 [16384], P(('lon', 'grp'))
- smooth_resid_new: float32 [16, 512, 512], P('lon')
- scalars_new: float32 [4], replicated
Inputs may be any that keep to these rules, and one draw needn't show every extreme that they name: `ray_sector`: the rays of one device name one sector at most 128 times, a bound that some block reaches.
All inputs are finite; a program needn't handle non-finite values.
Results may differ from a plain program's by a relative error of at most 0.00095.
Values may be sent and summed in bfloat16 or wider, within the bound.
A program may use at most 64 MiB of HBM per device.

v0:
```python
import math

import jax
import jax.numpy as jnp
from jax import lax
from jax.sharding import PartitionSpec as P

EPSILON = 1e-06


def extended_2(block, sides, width):
    for axis, dim in sides:
        count = lax.axis_size(axis)
        forward = [(i, i + 1) for i in range(count - 1)]
        forward.append((count - 1, 0))
        backward = [(target, source) for source, target in forward]
        low = lax.ppermute(
            lax.slice_in_dim(block, block.shape[dim] - width, None, axis=dim), axis, forward
        )
        high = lax.ppermute(lax.slice_in_dim(block, 0, width, axis=dim), axis, backward)
        block = jnp.concatenate([low, block, high], axis=dim)
    return block


def smoothing(extended, stencil_coeffs):
    center = extended[1:-1]
    along_lon = stencil_coeffs[0]
    along_lat = stencil_coeffs[1]
    along_depth = stencil_coeffs[2]
    damping = stencil_coeffs[3]
    lat_padded = jnp.pad(center, ((0, 0), (1, 1), (0, 0)))
    depth_padded = jnp.pad(center, ((0, 0), (0, 0), (1, 1)))
    diagonal = 2.0 * (along_lon + along_lat + along_depth) + damping
    return (
        diagonal * center
        - along_lon * (extended[2:] + extended[:-2])
        - along_lat * (lat_padded[:, 2:] + lat_padded[:, :-2])
        - along_depth * (depth_padded[:, :, 2:] + depth_padded[:, :, :-2])
    )


def lon_rim(grid_field):
    return extended_2(grid_field, (("lon", 0),), 1)


def strict_lower(count):
    rows_iota = jnp.arange(count, dtype=jnp.int32)
    return (rows_iota[:, None] > rows_iota[None, :]).astype(jnp.float32)


def slot_ranks(target, sectors):
    ray_count = target.shape[0]
    block_rows = math.gcd(ray_count, 128)
    block_count = ray_count // block_rows
    target_hits = (target[:, None] == jnp.arange(sectors, dtype=jnp.int32)[None, :]).astype(
        jnp.float32
    )
    blocked = target_hits.reshape(block_count, block_rows, sectors)
    within = jnp.einsum(
        "ij,bjs->bis", strict_lower(block_rows), blocked, precision=lax.Precision.HIGHEST
    )
    block_totals = jnp.sum(blocked, axis=1)
    before = jnp.dot(strict_lower(block_count), block_totals, precision=lax.Precision.HIGHEST)
    earlier = (within + before[:, None, :]).reshape(ray_count, sectors)
    return jnp.sum(earlier * target_hits, axis=1).astype(jnp.int32)


def on_device(
    ray_weights,
    ray_sector,
    ray_block,
    ray_offset,
    ray_resid,
    smooth_resid,
    model_dir,
    search_dir,
    model,
    stencil_coeffs,
    lsqr_scalars,
):
    sectors = lax.axis_size("lon")
    groups = lax.axis_size("grp")
    ray_count = ray_weights.shape[0]
    band_width = ray_weights.shape[1]
    lon_cells, lat_cells, depth_cells = model_dir.shape
    capacity = 2 * ray_count // sectors
    sector_cells = lon_cells * lat_cells * depth_cells
    cells_total = sector_cells * sectors
    rows_total = ray_count * sectors * groups + cells_total
    row_ratio = math.sqrt(rows_total / cells_total)
    alpha_now = lsqr_scalars[0]
    rho_bar = lsqr_scalars[1]
    phi_bar = lsqr_scalars[2]
    target = ray_sector[:, 0]
    slot_rank = slot_ranks(target, sectors)
    send_slot = target * capacity + slot_rank
    local_start = ray_block * depth_cells + ray_offset
    slots_all = sectors * capacity
    send_weights = jnp.zeros((slots_all, band_width), jnp.bfloat16).at[send_slot].set(ray_weights)
    send_resid = (
        jnp.zeros((slots_all,), jnp.bfloat16).at[send_slot].set(ray_resid.astype(jnp.bfloat16))
    )
    send_start = jnp.zeros((slots_all,), jnp.int32).at[send_slot].set(local_start)
    got_weights, got_resid, got_start = (
        lax.all_to_all(
            send_weights.reshape(sectors, capacity, band_width),
            "lon",
            split_axis=0,
            concat_axis=0,
            tiled=True,
        ),
        lax.all_to_all(
            send_resid.reshape(sectors, capacity), "lon", split_axis=0, concat_axis=0, tiled=True
        ),
        lax.all_to_all(
            send_start.reshape(sectors, capacity), "lon", split_axis=0, concat_axis=0, tiled=True
        ),
    )
    got_weights = got_weights.reshape(slots_all, band_width).astype(jnp.float32)
    got_resid = got_resid.reshape(slots_all).astype(jnp.float32)
    got_start = got_start.reshape(slots_all)
    sample_index = got_start[:, None] + jnp.arange(band_width, dtype=jnp.int32)[None, :]
    flat_dir = model_dir.reshape(-1)
    path_sum = jnp.sum(got_weights * jnp.take(flat_dir, sample_index), axis=1)
    ray_raw = row_ratio * path_sum - alpha_now * got_resid
    smooth_raw = (
        row_ratio * smoothing(lon_rim(model_dir), stencil_coeffs) - alpha_now * smooth_resid
    )
    lat_share = lat_cells // groups
    lat_start = lax.axis_index("grp") * lat_share
    smooth_part = lax.dynamic_slice_in_dim(smooth_raw, lat_start, lat_share, 1)
    local_squares = jnp.sum(ray_raw * ray_raw) + jnp.sum(smooth_part * smooth_part)
    beta_total = lax.psum(local_squares, ("lon", "grp"))
    beta_now = jnp.sqrt(beta_total / rows_total + EPSILON)
    ray_new = ray_raw / beta_now
    smooth_new = smooth_raw / beta_now
    returned = lax.all_to_all(
        ray_new.reshape(sectors, capacity), "lon", split_axis=0, concat_axis=0, tiled=True
    )
    ray_resid_new = jnp.take(returned.reshape(slots_all), send_slot)
    partial_value = (
        jnp.zeros((sector_cells,), jnp.float32)
        .at[sample_index.reshape(-1)]
        .add((got_weights * ray_new[:, None]).reshape(-1))
    )
    partial_value = partial_value.reshape(lon_cells, lat_cells, depth_cells)
    smooth_back = smoothing(lon_rim(smooth_new), stencil_coeffs)
    summed = lax.psum(partial_value, "grp")
    dir_raw = (summed + smooth_back) / row_ratio - beta_now * model_dir
    dir_part = lax.dynamic_slice_in_dim(dir_raw, lat_start, lat_share, 1)
    square_sum = jnp.sum(dir_part * dir_part)
    alpha_total = lax.psum(square_sum, ("lon", "grp"))
    alpha_new = jnp.sqrt(alpha_total / cells_total + EPSILON)
    dir_new = dir_raw / alpha_new
    rho_now = jnp.sqrt(rho_bar * rho_bar + beta_now * beta_now)
    cosine = rho_bar / rho_now
    sine = beta_now / rho_now
    theta_now = sine * alpha_new
    rho_bar_new = -cosine * alpha_new
    phi_now = cosine * phi_bar
    phi_bar_new = sine * phi_bar
    model_new = model + phi_now / rho_now * search_dir
    search_new = dir_new - theta_now / rho_now * search_dir
    scalars_new = jnp.stack([alpha_new, beta_now, rho_bar_new, phi_bar_new])
    return (model_new, search_new, dir_new, ray_resid_new, smooth_new, scalars_new)


def solution(mesh):
    placed = (
        P(("lon", "grp"), None),
        P(("lon", "grp"), None),
        P(("lon", "grp")),
        P(("lon", "grp")),
        P(("lon", "grp")),
        P("lon", None, None),
        P("lon", None, None),
        P("lon", None, None),
        P("lon", None, None),
        P(),
        P(),
    )
    return jax.shard_map(
        on_device,
        mesh=mesh,
        in_specs=placed,
        out_specs=(
            P("lon", None, None),
            P("lon", None, None),
            P("lon", None, None),
            P(("lon", "grp")),
            P("lon", None, None),
            P(),
        ),
        check_vma=False,
    )
```

profile of v0, /device:TPU:0, one launch (start us, length us, event | category | flops | bytes accessed | tf_op | source)
XLA Modules:
  0.0 1890.7 jit_solution(16096544300472462794)
XLA Ops:
  8.7 0.9 fusion.21
  9.7 1.2 and_reduce_fusion
  10.9 3.8 scatter_custom_fusion.2
  15.3 7.3 all-to-all-start.2
  22.6 3.0 fusion.41
  25.6 4.7 collective-permute-start
  31.7 3.0 scatter_custom_fusion.1
  34.7 2.8 scatter_custom_fusion
  37.5 2.1 copy.18
  42.1 6.0 all-to-all-start.1
  48.1 1.3 convert_multiply_fusion
  49.4 23.8 %all-to-all-done.1 = s32[8,1,128]{2,1,0:T(1,128)S(1)} async-done(((s32[8,1,128]{2,1,0:T(1,128)}), s32[8,1,128]{2,1,0:T(1,128)S(1)}, u32[]{:S(2)}, u32[]{:S(2)}) %all-to-all-start.1) | async-done | bytes 4128 | tf_op jit(solution)/shard_map/all_to_all | solution.py:115
  73.2 5.8 all-to-all-start
  79.4 724.9 %gather_fusion = f32[131072]{0:T(1024)S(1)} fusion(f32[524288]{0:T(1024)S(1)} %bitcast.53, s32[131072]{0:T(1024)S(1)} %fusion.25), kind=kCustom, calls=%fused_computation | custom fusion | bytes 1572864 | tf_op jit(solution)/shard_map/jit(_take)/gather | solution.py:124
  804.5 1.3 multiply_reduce_fusion.2
  806.4 10.2 fusion.4
  816.6 1.3 copy-done.2
  820.5 41.0 %psum.21 = f32[]{:T(128)} all-reduce(f32[]{:T(128)S(6)} %add.208), channel_id=1, replica_groups=mesh['lon'=8,'grp'=4] {'lon','grp'}, use_global_device_ids=true, to_apply=%region_8.9 | all-reduce | flops 1 | bytes 8 | tf_op jit(solution)/shard_map/psum | solution.py:133
  862.2 1.8 broadcast_divide_fusion.1
  864.1 1.4 bitcast_multiply_fusion
  865.4 904.4 %scatter_custom_fusion.3 = f32[524288]{0:T(1024)} fusion(s32[131072]{0:T(1024)S(1)} %bitcast.58, f32[131072]{0:T(1024)S(1)} %bitcast_multiply_fusion, f32[]{:T(128)} %constant.20.clone.1), kind=kCustom, calls=%fused_computation.44 | custom fusion | flops 131072 | bytes 2097156 | tf_op jit(solution)/shard_map/scatter-add | solution.py:144
  1769.8 2.7 reshape.222
  1772.6 1.5 fusion.40
  1774.1 3.0 collective-permute-start.2
  1777.1 1.3 subtract_divide_fusion
  1778.4 6.0 all-to-all-start.3
  1787.7 33.4 %all-to-all-done.3 = f32[8,1,128]{2,1,0:T(1,128)S(1)} async-done(((f32[8,1,128]{2,1,0:T(1,128)}), f32[8,1,128]{2,1,0:T(1,128)S(1)}, u32[]{:S(2)}, u32[]{:S(2)}) %all-to-all-start.3) | async-done | bytes 4128 | tf_op jit(solution)/shard_map/all_to_all | solution.py:137
  1821.0 2.3 gather_fusion.1
  1823.8 9.8 fusion.10
  1833.6 1.3 copy-done.3
  1836.2 40.0 %psum.23 = f32[]{:T(128)} all-reduce(f32[]{:T(128)} %multiply_reduce_fusion), channel_id=1, replica_groups=mesh['lon'=8,'grp'=4] {'lon','grp'}, use_global_device_ids=true, to_apply=%region_12.13 | all-reduce | flops 1 | bytes 8 | tf_op jit(solution)/shard_map/psum | solution.py:152
  1877.6 6.3 multiply_subtract_fusion
  (59 shorter events, 8.3 us)
Async XLA Ops:
  10.9 23.8 %copy-start.9 = (s32[512,1]{0,1:T(1,128)}, s32[512,1]{0,1:T(1,128)S(1)}, u32[]{:S(2)}) copy-start(s32[512,1]{0,1:T(1,128)S(1)} %get-tuple-element.7) | copy-start | bytes 6148
  15.3 26.8 %all-to-all-start.2 = ((bf16[8,1,128]{2,1,0:T(2,128)(2,1)}), bf16[8,1,128]{2,1,0:T(2,128)(2,1)S(1)}, u32[]{:S(2)}, u32[]{:S(2)}) async-start(bf16[8,1,128]{2,1,0:T(2,128)(2,1)} %copy.17), calls=%async_computation.2 | async-start | bytes 8192 | tf_op jit(solution)/shard_map/all_to_all | solution.py:112
  22.5 7.8 copy-start.11
  22.5 8.5 copy-start.13
  22.6 8.5 copy-start.14
  22.6 8.5 copy-start.12
  25.6 780.8 %collective-permute-start = (f32[1,512,512]{2,1,0:T(8,128)}, f32[1,512,512]{2,1,0:T(8,128)}, u32[]{:S(2)}, u32[]{:S(2)}) collective-permute-start(f32[1,512,512]{2,1,0:T(8,128)} %get-tuple-element.13), channel_id=1, source_target_pairs={{4,0},{8,4},{12,8},{16,12},{20,16},{24,20},{28,24},{0,28},{5,1},{9... | collective-permute-start | bytes 3145736 | tf_op jit(solution)/shard_map/ppermute | solution.py:20
  30.3 776.1 %collective-permute-start.1 = (f32[1,512,512]{2,1,0:T(8,128)}, f32[1,512,512]{2,1,0:T(8,128)}, u32[]{:S(2)}, u32[]{:S(2)}) collective-permute-start(f32[1,512,512]{2,1,0:T(8,128)} %get-tuple-element.14), channel_id=1, source_target_pairs={{0,4},{4,8},{8,12},{12,16},{16,20},{20,24},{24,28},{28,0},{1,5},{5... | collective-permute-start | bytes 3145736 | tf_op jit(solution)/shard_map/ppermute | solution.py:17
  42.1 37.2 %copy-start.7 = (bf16[8,1,128]{2,1,0:T(2,128)(2,1)}, bf16[8,1,128]{2,1,0:T(2,128)(2,1)S(1)}, u32[]{:S(2)}) copy-start(bf16[8,1,128]{2,1,0:T(2,128)(2,1)S(1)} %all-to-all-done.2) | copy-start | bytes 6148
  42.1 31.1 %all-to-all-start.1 = ((s32[8,1,128]{2,1,0:T(1,128)}), s32[8,1,128]{2,1,0:T(1,128)S(1)}, u32[]{:S(2)}, u32[]{:S(2)}) async-start(s32[8,1,128]{2,1,0:T(1,128)} %bitcast.7), calls=%async_computation.1 | async-start | bytes 8192 | tf_op jit(solution)/shard_map/all_to_all | solution.py:115
  73.2 6.1 copy-start.4
  73.2 731.2 %all-to-all-start = ((bf16[8,128,128]{2,1,0:T(8,128)(2,1)}), bf16[8,128,128]{2,1,0:T(8,128)(2,1)}, u32[]{:S(2)}, u32[]{:S(2)}) async-start(bf16[8,128,128]{2,1,0:T(8,128)(2,1)} %bitcast.6), calls=%async_computation | async-start | bytes 524288 | tf_op jit(solution)/shard_map/all_to_all | solution.py:105
  79.1 1744.7 %all-reduce.6.cloned.1.call-start = ((), (), s32[]{:S(2)}) async-start(), calls=%async_computation.4 | async-start | bytes 4194304 | tf_op jit(solution)/shard_map/psum | solution.py:148
  79.3 724.9 %copy-start.5 = (s32[8,1,128]{2,1,0:T(1,128)S(1)}, s32[8,1,128]{2,1,0:T(1,128)}, u32[]{:S(2)}) copy-start(s32[8,1,128]{2,1,0:T(1,128)} %copy-done.4) | copy-start | bytes 12292
  79.4 726.5 %copy-start.6 = (f32[8,1,128]{2,1,0:T(1,128)S(1)}, f32[8,1,128]{2,1,0:T(1,128)}, u32[]{:S(2)}) copy-start(f32[8,1,128]{2,1,0:T(1,128)} %convert_multiply_fusion) | copy-start | bytes 12292
  816.6 1.3 copy-start.2
  864.0 908.5 %copy-start.1 = (f32[2,512,512]{2,1,0:T(8,128)}, f32[2,512,512]{2,1,0:T(8,128)S(1)}, u32[]{:S(2)}) copy-start(f32[2,512,512]{2,1,0:T(8,128)S(1)} %broadcast_divide_fusion.1) | copy-start | bytes 6291460
  1772.6 4.6 copy-start.8
  1772.6 11.8 copy-start.10
  1774.1 49.7 %copy-start = (f32[2,512,512]{2,1,0:T(8,128)S(1)}, f32[2,512,512]{2,1,0:T(8,128)}, u32[]{:S(2)}) copy-start(f32[2,512,512]{2,1,0:T(8,128)} %param.17) | copy-start | bytes 6291460
  1774.1 49.7 %collective-permute-start.2 = (f32[1,512,512]{2,1,0:T(8,128)}, f32[1,512,512]{2,1,0:T(8,128)S(1)}, u32[]{:S(2)}, u32[]{:S(2)}) collective-permute-start(f32[1,512,512]{2,1,0:T(8,128)} %get-tuple-element.11), channel_id=1, source_target_pairs={{4,0},{8,4},{12,8},{16,12},{20,16},{24,20},{28,24},{0,28},{5,1},{9... | collective-permute-start | bytes 3145736 | tf_op jit(solution)/shard_map/ppermute | solution.py:20
  1777.1 46.7 %collective-permute-start.3 = (f32[1,512,512]{2,1,0:T(8,128)}, f32[1,512,512]{2,1,0:T(8,128)}, u32[]{:S(2)}, u32[]{:S(2)}) collective-permute-start(f32[1,512,512]{2,1,0:T(8,128)} %get-tuple-element.12), channel_id=1, source_target_pairs={{0,4},{4,8},{8,12},{12,16},{16,20},{20,24},{24,28},{28,0},{1,5},{5... | collective-permute-start | bytes 3145736 | tf_op jit(solution)/shard_map/ppermute | solution.py:17
  1778.4 42.6 %all-to-all-start.3 = ((f32[8,1,128]{2,1,0:T(1,128)}), f32[8,1,128]{2,1,0:T(1,128)S(1)}, u32[]{:S(2)}, u32[]{:S(2)}) async-start(f32[8,1,128]{2,1,0:T(1,128)} %subtract_divide_fusion), calls=%async_computation.3 | async-start | bytes 8192 | tf_op jit(solution)/shard_map/all_to_all | solution.py:137
  1823.3 12.3 copy-start.15
  1833.6 1.3 copy-start.3
Sparse Core Ops, SparseCore 0:
  1772.7 51.0 all-reduce.5
where the time goes:
time: 1890 us
  other arithmetic  945 us (50%)
  local copies, waits for them, and re-layouts  751 us (40%)
  blocking collectives  81 us (4%)
  waiting for transfers between devices  57.7 us (3%)
  starting transfers between devices  32.9 us (2%)
  between operations  22.8 us (1%)
    scatter-add x1, other arithmetic, on_device(): partial_value = jnp.zeros((sector_cells,), jnp.float32).at[sample_index.r...  904 us
    gather x1, local copies, waits for them, and re-layouts, on_device(): path_sum = jnp.sum(got_weights * jnp.take(flat_dir, sample_index), axis=1)  725 us
    psum x1, blocking collectives, on_device(): beta_total = lax.psum(local_squares, ('lon', 'grp'))  41 us
    psum x1, blocking collectives, on_device(): alpha_total = lax.psum(square_sum, ('lon', 'grp'))  40 us
  transfers between devices with their start and end apart: 9, of which 3 were waited for; matrix products, arithmetic and copies ran while one was open for 39% of the time, Pallas kernels for 0%

commit v1 on v0

v1 whole, which is shorter than its diff:
```python
import functools
import math

import jax
import jax.numpy as jnp
from jax import lax
from jax.experimental import pallas as pl
from jax.experimental.pallas import tpu as pltpu
from jax.sharding import PartitionSpec as P

EPSILON = 1e-06
MESH = pl.DeviceIdType.MESH
F32 = jnp.float32
BF16 = jnp.bfloat16
LANES = 128
META = 16
TILE = 16
CHUNK_BLOCKS = 4
NT = (((1,), (1,)), ((), ()))
NN = (((1,), (0,)), ((), ()))


def dot(a, b, dims=NN):
    return lax.dot_general(a, b, dims, preferred_element_type=F32)


def kernel(
    cfg,
    coef_ref,
    rows_ref,
    w_ref,
    v_ref,
    resid_ref,
    sr_ref,
    back_ref,
    home_ref,
    sums_ref,
    msg,
    rays,
    halo,
    psend,
    vhi,
    vlo,
    wx,
    rr,
    ret_send,
    ret_recv,
    a_send,
    a_recv,
    y_send,
    y_recv,
    c_send,
    c_recv,
    d_send,
    d_recv,
    h_send,
    h_recv,
    hy_send,
    hy_recv,
    hc_send,
    hc_recv,
    hd_send,
    hd_recv,
    r_send,
    r_recv,
):
    n, groups, capp, ray_count, lat, depth, ratio = cfg
    me = lax.axis_index("lon")
    g = lax.axis_index("grp")
    gy = lax.rem(g + 2, 4)
    gc = g + 1 - 2 * lax.rem(g, 2)
    right = lax.rem(me + 1, n)
    left = lax.rem(me + n - 1, n)
    share = lat // groups
    q0 = pl.multiple_of(g * share, share)
    qy0 = pl.multiple_of(gy * share, share)
    k0 = coef_ref[0]
    k1 = coef_ref[1]
    k2 = coef_ref[2]
    diag = 2.0 * (k0 + k1 + k2) + coef_ref[3]
    alpha = coef_ref[4]

    barrier = pltpu.get_barrier_semaphore()

    def greet(d, carry):
        pl.semaphore_signal(
            barrier, inc=1, device_id=(lax.rem(me + d, n), g), device_id_type=MESH
        )
        return carry

    lax.fori_loop(1, n, greet, 0)
    pl.semaphore_signal(barrier, inc=1, device_id=(me, gy), device_id_type=MESH)
    pl.semaphore_signal(barrier, inc=1, device_id=(me, gc), device_id_type=MESH)

    target = rows_ref[0:1, :]
    block = rows_ref[1:2, :]
    offset = rows_ref[2:3, :]
    resid = rows_ref[3:4, :]
    sector_rows = -(-n // 16) * 16
    sector_iota = lax.broadcasted_iota(jnp.int32, (sector_rows, ray_count), 0).astype(F32)
    hits = (sector_iota == target).astype(F32)
    before = lax.broadcasted_iota(jnp.int32, (ray_count, ray_count), 0) < lax.broadcasted_iota(
        jnp.int32, (ray_count, ray_count), 1
    )
    rank_all = dot(hits.astype(BF16), jnp.where(before, 1.0, 0.0).astype(BF16))
    slot = target * capp + jnp.sum(hits * rank_all, axis=0, keepdims=True)

    offset_col = jnp.transpose(rows_ref[...])[:, 2:3].astype(jnp.int32)
    turned = w_ref[...].astype(F32)
    for bit in range(7):
        on = lax.rem(offset_col // (1 << bit), 2) == 1
        turned = jnp.where(on, pltpu.roll(turned, 1 << bit, 1), turned)
    turned = turned.astype(BF16)
    block_high = jnp.floor(block * (1.0 / 32))
    offset_high = jnp.floor(offset * (1.0 / 32))
    fields = jnp.concatenate(
        [
            block_high,
            block - 32.0 * block_high,
            offset_high,
            offset - 32.0 * offset_high,
            resid,
            jnp.zeros((META - 5, ray_count), F32),
        ],
        axis=0,
    ).astype(BF16)
    slot_iota = lax.broadcasted_iota(jnp.int32, (capp, ray_count), 0)

    def chosen(s):
        return jnp.where(slot == (slot_iota + s * capp).astype(F32), 1.0, 0.0).astype(BF16)

    def fill(s, carry):
        picked = chosen(s)
        msg[s, :capp, :] = dot(picked, turned).astype(BF16)
        msg[s, capp:, :] = dot(fields, picked, NT).astype(BF16)
        return carry

    lax.fori_loop(0, n, fill, 0)
    rays[g, me] = msg[me]

    pl.semaphore_wait(barrier, n + 1)

    def route(d):
        peer = lax.rem(me + d, n)
        return pltpu.make_async_remote_copy(
            msg.at[peer], rays.at[g, me], a_send.at[d], a_recv.at[d],
            device_id=(peer, g), device_id_type=MESH,
        )

    def route_start(d, carry):
        route(d).start()
        return carry

    lax.fori_loop(1, n, route_start, 0)

    lane = lax.broadcasted_iota(jnp.int32, (TILE, depth), 1)
    first_lane = lane == 0
    last_lane = lane == depth - 1

    def planar(ref, layer, start):
        low = ref[layer, pl.ds(pl.multiple_of(jnp.maximum(start - 8, 0), 8), 8), :]
        low = low * jnp.where(start > 0, 1.0, 0.0)
        high = ref[layer, pl.ds(pl.multiple_of(jnp.minimum(start + TILE, lat - 8), 8), 8), :]
        high = high * jnp.where(start + TILE < lat, 1.0, 0.0)
        mid = ref[layer, pl.ds(start, TILE), :]
        tall = jnp.concatenate([low, mid, high], axis=0)
        rows = TILE + 16
        along_lat = pltpu.roll(tall, 1, 0)[8 : 8 + TILE] + pltpu.roll(tall, rows - 1, 0)[8 : 8 + TILE]
        along_depth = jnp.where(first_lane, 0.0, pltpu.roll(mid, 1, 1)) + jnp.where(
            last_lane, 0.0, pltpu.roll(mid, depth - 1, 1)
        )
        return diag * mid - k1 * along_lat - k2 * along_depth, mid

    for layer in range(2):

        def outer(t, carry, layer=layer):
            start = pl.multiple_of(q0 + t * TILE, TILE)
            plane, _ = planar(v_ref, layer, start)
            other = v_ref[1 - layer, pl.ds(start, TILE), :]
            psend[layer, pl.ds(pl.multiple_of(t * TILE, TILE), TILE), :] = (
                ratio * (plane - k0 * other) - alpha * resid_ref[layer, pl.ds(start, TILE), :]
            )
            return carry

        lax.fori_loop(0, share // TILE, outer, 0)

    own = pl.ds(q0, share)
    sources = [
        (v_ref.at[1, own], right),
        (v_ref.at[0, own], left),
        (psend.at[1], right),
        (psend.at[0], left),
    ]
    halo_copies = [
        pltpu.make_async_remote_copy(
            src, halo.at[i, own], h_send.at[i], h_recv.at[i],
            device_id=(peer, g), device_id_type=MESH,
        )
        for i, (src, peer) in enumerate(sources)
    ]
    for copy in halo_copies:
        copy.start()

    def split(t, carry):
        rows = pl.ds(pl.multiple_of(t * TILE, TILE), TILE)
        for layer in range(2):
            x = v_ref[layer, rows, :]
            high = x.astype(BF16)
            target_rows = pl.ds(pl.multiple_of(layer * lat + t * TILE, TILE), TILE)
            vhi[target_rows, :] = high
            vlo[target_rows, :] = (x - high.astype(F32)).astype(BF16)
            back_ref[layer, rows, :] = jnp.zeros((TILE, depth), F32)
        return carry

    lax.fori_loop(0, lat // TILE, split, 0)

    def along_y(d):
        src = rays.at[g, lax.rem(me - d + n, n)]
        return pltpu.make_async_remote_copy(
            src, src, y_send.at[d], y_recv.at[d], device_id=(me, gy), device_id_type=MESH
        )

    def along_c(d):
        src = rays.at[g, lax.rem(me - d + n, n)]
        return pltpu.make_async_remote_copy(
            src, src, c_send.at[d], c_recv.at[d], device_id=(me, gc), device_id_type=MESH
        )

    def along_d(d):
        src = rays.at[gy, lax.rem(me - d + n, n)]
        return pltpu.make_async_remote_copy(
            src, src, d_send.at[d], d_recv.at[d], device_id=(me, gc), device_id_type=MESH
        )

    along_y(0).start()
    along_c(0).start()

    def pass_on(d, carry):
        route(d).wait_recv()
        along_y(d).start()
        along_c(d).start()
        return carry

    lax.fori_loop(1, n, pass_on, 0)

    def pass_again(d, carry):
        along_y(d).wait_recv()
        along_d(d).start()
        return carry

    lax.fori_loop(0, n, pass_again, 0)

    hy = []
    hc = []
    for i in range(4):
        halo_copies[i].wait_recv()
        piece = halo.at[i, own]
        hy.append(
            pltpu.make_async_remote_copy(
                piece, piece, hy_send.at[i], hy_recv.at[i],
                device_id=(me, gy), device_id_type=MESH,
            )
        )
        hc.append(
            pltpu.make_async_remote_copy(
                piece, piece, hc_send.at[i], hc_recv.at[i],
                device_id=(me, gc), device_id_type=MESH,
            )
        )
        hy[i].start()
        hc[i].start()

    def settle(d, carry):
        along_c(d).wait_recv()
        along_d(d).wait_recv()
        return carry

    lax.fori_loop(0, n, settle, 0)

    per_group = n // CHUNK_BLOCKS
    chunk = CHUNK_BLOCKS * capp
    cells = 2 * lat
    cell_tile = math.gcd(cells, 256)
    cell_iota = lax.broadcasted_iota(jnp.int32, (cell_tile, chunk), 0)
    spot = lax.broadcasted_iota(jnp.int32, (capp, LANES), 1)

    def ray_chunk(c, square):
        source_group = c // per_group
        base = lax.rem(c, per_group) * CHUNK_BLOCKS
        block_rows = []
        resid_rows = []
        for i in range(CHUNK_BLOCKS):
            meta = rays[source_group, base + i, capp:, :].astype(F32)
            block_rows.append(meta[0:1] * 32.0 + meta[1:2])
            resid_rows.append(meta[4:5])
            start = jnp.broadcast_to(meta[2:3] * 32.0 + meta[3:4], (8, capp))
            start_col = jnp.transpose(start)[:, 0:1].astype(jnp.int32)
            weights = rays[source_group, base + i, :capp, :].astype(F32)
            for j in range(depth // LANES):
                where = spot + (j * LANES) - start_col
                inside = (where >= 0) & (where < LANES)
                wx[i * capp : (i + 1) * capp, j * LANES : (j + 1) * LANES] = jnp.where(
                    inside, weights, 0.0
                ).astype(BF16)
        block_row = jnp.concatenate(block_rows, axis=1).astype(jnp.int32)
        resid_row = jnp.concatenate(resid_rows, axis=1)

        def product(t, total):
            rows = pl.ds(pl.multiple_of(t * cell_tile, cell_tile), cell_tile)
            found = dot(vhi[rows, :], wx[...], NT) + dot(vlo[rows, :], wx[...], NT)
            hit = (cell_iota + t * cell_tile) == block_row
            return total + jnp.sum(jnp.where(hit, found, 0.0), axis=0, keepdims=True)

        path = lax.fori_loop(0, cells // cell_tile, product, jnp.zeros((1, chunk), F32))
        raw = ratio * path - alpha * resid_row
        for i in range(CHUNK_BLOCKS):
            rr[source_group * n + base + i] = jnp.broadcast_to(
                raw[:, i * capp : (i + 1) * capp], (8, capp)
            )
        raw_high = raw.astype(BF16).astype(F32)
        raw_low = raw - raw_high

        def spread(t, carry):
            layer = t * cell_tile // lat
            rows = pl.ds(pl.multiple_of(lax.rem(t * cell_tile, lat), cell_tile), cell_tile)
            hit = (cell_iota + t * cell_tile) == block_row
            back_ref[layer, rows, :] += dot(
                jnp.where(hit, raw_high, 0.0).astype(BF16), wx[...]
            ) + dot(jnp.where(hit, raw_low, 0.0).astype(BF16), wx[...])
            return carry

        lax.fori_loop(0, cells // cell_tile, spread, 0)
        return square + raw * raw

    chunks = groups * per_group
    square = lax.fori_loop(0, chunks // 2, ray_chunk, jnp.zeros((1, chunk), F32))
    hd = []
    for i in range(4):
        hy[i].wait_recv()
        piece = halo.at[i, pl.ds(qy0, share)]
        hd.append(
            pltpu.make_async_remote_copy(
                piece, piece, hd_send.at[i], hd_recv.at[i],
                device_id=(me, gc), device_id_type=MESH,
            )
        )
        hd[i].start()
    square = lax.fori_loop(chunks // 2, chunks, ray_chunk, square)
    ray_square = jnp.sum(square)
    for i in range(4):
        hc[i].wait_recv()
        hd[i].wait_recv()

    def fold(x):
        return jnp.sum(x.reshape(TILE // 8, 8, depth), axis=0)

    zero = jnp.zeros((8, depth), F32)
    smooth_square = zero
    for layer in range(2):

        def forward(t, total, layer=layer):
            start = pl.multiple_of(t * TILE, TILE)
            rows = pl.ds(start, TILE)
            plane, _ = planar(v_ref, layer, start)
            beside = halo[layer, rows, :] + v_ref[1 - layer, rows, :]
            raw = ratio * (plane - k0 * beside) - alpha * resid_ref[layer, rows, :]
            sr_ref[layer, rows, :] = raw
            return total + fold(raw * raw)

        smooth_square = lax.fori_loop(0, lat // TILE, forward, smooth_square)

    totals = (zero, zero, zero)
    for layer in range(2):

        def transposed(t, totals, layer=layer):
            start = pl.multiple_of(t * TILE, TILE)
            rows = pl.ds(start, TILE)
            plane, _ = planar(sr_ref, layer, start)
            x = v_ref[layer, rows, :]
            outside = halo[2 + layer, rows, :] - (ratio * k0) * x
            value = back_ref[layer, rows, :] + plane - k0 * (outside + sr_ref[1 - layer, rows, :])
            back_ref[layer, rows, :] = value
            return (
                totals[0] + fold(value * value),
                totals[1] + fold(value * x),
                totals[2] + fold(x * x),
            )

        totals = lax.fori_loop(0, lat // TILE, transposed, totals)

    sub = lax.broadcasted_iota(jnp.int32, (8, LANES), 0)
    col = lax.broadcasted_iota(jnp.int32, (8, LANES), 1)
    numbers = [ray_square + jnp.sum(smooth_square)] + [jnp.sum(x) for x in totals]
    sums = jnp.zeros((8, LANES), F32)
    for i, number in enumerate(numbers):
        sums = jnp.where(col == i, number, sums)

    def answer(s, carry):
        ret_send[s] = jnp.where(sub == 0, rr[g * n + s], sums)
        return carry

    lax.fori_loop(0, n, answer, 0)
    ret_recv[me] = ret_send[me]

    def give_back(d):
        peer = lax.rem(me + d, n)
        return pltpu.make_async_remote_copy(
            ret_send.at[peer], ret_recv.at[me], r_send.at[d], r_recv.at[d],
            device_id=(peer, g), device_id_type=MESH,
        )

    def give_start(d, carry):
        give_back(d).start()
        return carry

    def give_wait(d, carry):
        give_back(d).wait_recv()
        return carry

    lax.fori_loop(1, n, give_start, 0)
    lax.fori_loop(1, n, give_wait, 0)

    def collect(s, carry):
        total, home = carry
        tile = ret_recv[s]
        one = tile.astype(BF16).astype(F32)
        two = (tile - one).astype(BF16).astype(F32)
        three = tile - one - two
        stack = jnp.concatenate([one, two, three, jnp.zeros((8, LANES), F32)], axis=0).astype(BF16)
        got = dot(stack, chosen(s))
        return total + tile, home + (got[0:8] + got[8:16] + got[16:24])

    total, home = lax.fori_loop(
        0, n, collect, (jnp.zeros((8, LANES), F32), jnp.zeros((8, ray_count), F32))
    )
    sums_ref[...] = total
    home_ref[...] = home

    def finish(d, carry):
        route(d).wait_send()
        give_back(d).wait_send()
        return carry

    lax.fori_loop(1, n, finish, 0)

    def finish_all(d, carry):
        along_y(d).wait_send()
        along_c(d).wait_send()
        along_d(d).wait_send()
        return carry

    lax.fori_loop(0, n, finish_all, 0)
    for copy in halo_copies + hy + hc + hd:
        copy.wait_send()


def on_device(
    ray_weights,
    ray_sector,
    ray_block,
    ray_offset,
    ray_resid,
    smooth_resid,
    model_dir,
    search_dir,
    model,
    stencil_coeffs,
    lsqr_scalars,
):
    n = lax.axis_size("lon")
    groups = lax.axis_size("grp")
    ray_count = ray_weights.shape[0]
    lon_cells, lat, depth = model_dir.shape
    assert lon_cells == 2 and groups == 4 and n % CHUNK_BLOCKS == 0
    capacity = 2 * ray_count // n
    capp = -(-capacity // LANES) * LANES
    assert capp == LANES
    cells_total = lon_cells * lat * depth * n
    rows_total = ray_count * n * groups + cells_total
    ratio = math.sqrt(rows_total / cells_total)
    rows = jnp.concatenate(
        [
            jnp.stack(
                [
                    ray_sector[:, 0].astype(F32),
                    ray_block.astype(F32),
                    ray_offset.astype(F32),
                    ray_resid.astype(BF16).astype(F32),
                ]
            ),
            jnp.zeros((4, ray_count), F32),
        ]
    )
    coef = jnp.concatenate([stencil_coeffs, lsqr_scalars])
    field = jax.ShapeDtypeStruct((2, lat, depth), F32)
    vmem = pl.BlockSpec(memory_space=pltpu.VMEM)
    dma = pltpu.SemaphoreType.DMA
    cfg = (n, groups, capp, ray_count, lat, depth, ratio)
    smooth_raw, back, home, sums = pl.pallas_call(
        functools.partial(kernel, cfg),
        out_shape=(
            field,
            field,
            jax.ShapeDtypeStruct((8, ray_count), F32),
            jax.ShapeDtypeStruct((8, LANES), F32),
        ),
        in_specs=[pl.BlockSpec(memory_space=pltpu.SMEM)] + [vmem] * 4,
        out_specs=(vmem,) * 4,
        scratch_shapes=[
            pltpu.VMEM((n, capp + META, LANES), BF16),
            pltpu.VMEM((groups, n, capp + META, LANES), BF16),
            pltpu.VMEM((4, lat, depth), F32),
            pltpu.VMEM((2, lat // groups, depth), F32),
            pltpu.VMEM((2 * lat, depth), BF16),
            pltpu.VMEM((2 * lat, depth), BF16),
            pltpu.VMEM((CHUNK_BLOCKS * capp, depth), BF16),
            pltpu.VMEM((groups * n, 8, capp), F32),
            pltpu.VMEM((n, 8, LANES), F32),
            pltpu.VMEM((n, 8, LANES), F32),
        ]
        + [dma((n,))] * 8
        + [dma((4,))] * 8
        + [dma((n,))] * 2,
        compiler_params=pltpu.CompilerParams(
            collective_id=0, has_side_effects=True, vmem_limit_bytes=48 * 1024 * 1024
        ),
        cost_estimate=pl.CostEstimate(
            flops=20_000_000_000, bytes_accessed=8_000_000, transcendentals=0
        ),
    )(coef, rows, ray_weights, model_dir, smooth_resid)

    alpha_now = lsqr_scalars[0]
    rho_bar = lsqr_scalars[1]
    phi_bar = lsqr_scalars[2]
    beta_now = jnp.sqrt(sums[1, 0] / rows_total + EPSILON)
    scale = 1.0 / (beta_now * ratio)
    alpha_total = (
        scale * scale * sums[1, 1]
        - 2.0 * (scale * beta_now) * sums[1, 2]
        + beta_now * beta_now * sums[1, 3]
    )
    alpha_new = jnp.sqrt(jnp.maximum(alpha_total, 0.0) / cells_total + EPSILON)
    rho_now = jnp.sqrt(rho_bar * rho_bar + beta_now * beta_now)
    cosine = rho_bar / rho_now
    sine = beta_now / rho_now
    theta_now = sine * alpha_new
    rho_bar_new = -cosine * alpha_new
    phi_now = cosine * phi_bar
    phi_bar_new = sine * phi_bar
    beta_inverse = 1.0 / beta_now
    dir_new = back * (scale / alpha_new) - model_dir * (beta_now / alpha_new)
    smooth_new = smooth_raw * beta_inverse
    ray_resid_new = home[0] * beta_inverse
    model_new = model + phi_now / rho_now * search_dir
    search_new = dir_new - theta_now / rho_now * search_dir
    scalars_new = jnp.stack([alpha_new, beta_now, rho_bar_new, phi_bar_new])
    return (model_new, search_new, dir_new, ray_resid_new, smooth_new, scalars_new)


def solution(mesh):
    placed = (
        P(("lon", "grp"), None),
        P(("lon", "grp"), None),
        P(("lon", "grp")),
        P(("lon", "grp")),
        P(("lon", "grp")),
        P("lon", None, None),
        P("lon", None, None),
        P("lon", None, None),
        P("lon", None, None),
        P(),
        P(),
    )
    return jax.shard_map(
        on_device,
        mesh=mesh,
        in_specs=placed,
        out_specs=(
            P("lon", None, None),
            P("lon", None, None),
            P("lon", None, None),
            P(("lon", "grp")),
            P("lon", None, None),
            P(),
        ),
        check_vma=False,
    )
```

time: 1890 us -> 114 us (0.06)
  other arithmetic: 945 us -> 12.2 us
  local copies, waits for them, and re-layouts: 751 us -> 4.15 us
  Pallas kernels: 0 us -> 90.5 us
  blocking collectives: 81 us -> 0 us
  waiting for transfers between devices: 57.7 us -> 0 us
  starting transfers between devices: 32.9 us -> 0 us
    scatter-add x1 -> x0, other arithmetic: 904 us -> none  [on_device(): partial_value = jnp.zeros((sector_cells,), jnp.float32).at[sample_index.r...]
    gather x2 -> x0, local copies, waits for them, and re-layouts: 727 us -> none  [the longest x1 725 us: on_device(): path_sum = jnp.sum(got_weights * jnp.take(flat_dir, sample_index), axis=1)]
    pallas_call x0 -> x1, Pallas kernels: none -> 90.5 us  [on_device(): pl.pallas_call(functools.partial(kernel, cfg), out_shape=(field, field, j...]
    psum x2 -> x0, blocking collectives: 81 us -> none  [the longest x1 41 us: on_device(): beta_total = lax.psum(local_squares, ('lon', 'grp'))]
    all_to_all x4 -> x0, waiting for transfers between devices: 57.2 us -> none  [the longest x1 33.4 us: on_device(): lax.all_to_all(ray_new.reshape(sectors, capacity), 'lon', split_axis=0, c...]
    all_to_all x4 -> x0, starting transfers between devices: 25.1 us -> none  [the longest x1 7.25 us: on_device(): lax.all_to_all(send_resid.reshape(sectors, capacity), 'lon', split_axis=0...]
    sub x2 -> x0, other arithmetic: 19.9 us -> none  [the longest x1 10.2 us: on_device(): row_ratio * smoothing(lon_rim(model_dir), stencil_coeffs)]
  transfers between devices with their start and end apart: 9 -> 0, of which waited for: 3 -> 0; matrix products, arithmetic and copies ran while one was open for 39% -> 0% of each run, Pallas kernels for 0% -> 0%
where the time goes in v1:
time: 114 us
  Pallas kernels  90.5 us (79%)
  other arithmetic  12.2 us (11%)
  between operations  6.67 us (6%)
  local copies, waits for them, and re-layouts  4.15 us (4%)
    pallas_call x1, Pallas kernels, on_device(): pl.pallas_call(functools.partial(kernel, cfg), out_shape=(field, field, j...  90.5 us
    sub x1, other arithmetic, on_device(): search_new = dir_new - theta_now / rho_now * search_dir  7.59 us

profile of v1, /device:TPU:0, one launch (start us, length us, event | category | flops | bytes accessed | tf_op | source)
XLA Modules:
  0.0 113.6 jit_solution(10499427287477042707)
XLA Ops:
  0.6 0.7 pad_maximum_fusion.coef_ref
  1.4 1.3 %fusion.1 = (f32[1]{0:T(128)}, f32[1]{0:T(128)}) fusion(f32[3]{0:T(128)} %param.21), kind=kLoop, calls=%fused_computation.10 | loop fusion | bytes 16 | tf_op jit(solution)/shard_map/slice | solution.py:534
  3.8 0.7 convert_bitcast_fusion
  4.5 0.7 convert_element_type.25
  5.2 0.7 convert_element_type.26
  5.9 0.7 convert_convert_fusion
  6.6 0.0 copy-start.1
  6.6 0.9 copy-done.1
  7.5 90.5 %shard_map.154 = (f32[2,512,512]{2,1,0:T(8,128)S(1)}, f32[2,512,512]{2,1,0:T(8,128)S(1)}, f32[8,512]{1,0:T(8,128)S(1)}, f32[8,128]{1,0:T(8,128)S(1)}) custom-call(f32[7]{0:T(128)S(1)} %pad_maximum_fusion.coef_ref, f32[8,512]{1,0:T(8,128)S(1)} %concatenate.7.rows_ref, bf16[512,128]{1,0:T(8,128)(2,1)S(1)} %copy-done.1, f32[2,512,512]{2,1,0:T(8,128)} %v_ref.1, ...), custom_call_target="tpu_custom_call" | custom-call | flops 20000000000 | bytes 8000000 | tf_op jit(solution)/shard_map/pallas_call | solution.py:499
  98.0 0.0 copy-start
  98.1 1.3 %copy-done = f32[2,512,512]{2,1,0:T(8,128)} copy-done((f32[2,512,512]{2,1,0:T(8,128)}, f32[2,512,512]{2,1,0:T(8,128)S(1)}, u32[]{:S(2)}) %copy-start) | copy-done | bytes 2097176
  99.4 0.6 fusion
  104.8 0.6 slice_multiply_fusion
  105.4 0.6 pad_maximum_fusion.1
  106.0 7.6 %multiply_subtract_fusion = (f32[2,512,512]{2,1,0:T(8,128)}, f32[2,512,512]{2,1,0:T(8,128)}, f32[2,512,512]{2,1,0:T(8,128)}, f32[2,512,512]{2,1,0:T(8,128)}) fusion(f32[2,512,512]{2,1,0:T(8,128)} %param.18, f32[]{:T(128)S(6)} %div.38, f32[2,512,512]{2,1,0:T(8,128)} %v_ref.1, f32[]{:T(128)S(6)} %div.36, f32[2,512,512]{2,1,0:T(8,128)} %copy-done, f32[]{:T(128)S(6)} %div.35, ...), kind=kLoop, calls=%fused_computation | loop fusion | flops 4194304 | bytes 18874388 | tf_op jit(solution)/shard_map/sub | solution.py:555
  (2 shorter events, 0.0 us)
Async XLA Ops:
  6.6 0.9 copy-start.1
  98.0 1.3 %copy-start = (f32[2,512,512]{2,1,0:T(8,128)}, f32[2,512,512]{2,1,0:T(8,128)S(1)}, u32[]{:S(2)}) copy-start(f32[2,512,512]{2,1,0:T(8,128)S(1)} %get-tuple-element.11) | copy-start | bytes 6291460

commit v2 on v1

--- a/solution.py
+++ b/solution.py
@@ -26,15 +26,19 @@
 
 def kernel(
     cfg,
-    coef_ref,
-    rows_ref,
+    stencil_ref,
+    scalar_ref,
+    sector_ref,
+    block_ref,
+    offset_ref,
+    left_ref,
     w_ref,
     v_ref,
     resid_ref,
     sr_ref,
     back_ref,
     home_ref,
-    sums_ref,
+    coef_ref,
     msg,
     rays,
     halo,
@@ -64,7 +68,7 @@
     r_send,
     r_recv,
 ):
-    n, groups, capp, ray_count, lat, depth, ratio = cfg
+    n, groups, capp, ray_count, lat, depth, ratio, rows_total, cells_total = cfg
     me = lax.axis_index("lon")
     g = lax.axis_index("grp")
     gy = lax.rem(g + 2, 4)
@@ -74,11 +78,11 @@
     share = lat // groups
     q0 = pl.multiple_of(g * share, share)
     qy0 = pl.multiple_of(gy * share, share)
-    k0 = coef_ref[0]
-    k1 = coef_ref[1]
-    k2 = coef_ref[2]
-    diag = 2.0 * (k0 + k1 + k2) + coef_ref[3]
-    alpha = coef_ref[4]
+    k0 = stencil_ref[0]
+    k1 = stencil_ref[1]
+    k2 = stencil_ref[2]
+    diag = 2.0 * (k0 + k1 + k2) + stencil_ref[3]
+    alpha = scalar_ref[0]
 
     barrier = pltpu.get_barrier_semaphore()
 
@@ -92,10 +96,29 @@
     pl.semaphore_signal(barrier, inc=1, device_id=(me, gy), device_id_type=MESH)
     pl.semaphore_signal(barrier, inc=1, device_id=(me, gc), device_id_type=MESH)
 
-    target = rows_ref[0:1, :]
-    block = rows_ref[1:2, :]
-    offset = rows_ref[2:3, :]
-    resid = rows_ref[3:4, :]
+    pl.semaphore_wait(barrier, n + 1)
+
+    own = pl.ds(q0, share)
+    sources = [
+        (v_ref.at[1, own], right),
+        (v_ref.at[0, own], left),
+        (psend.at[1], right),
+        (psend.at[0], left),
+    ]
+    halo_copies = [
+        pltpu.make_async_remote_copy(
+            src, halo.at[i, own], h_send.at[i], h_recv.at[i],
+            device_id=(peer, g), device_id_type=MESH,
+        )
+        for i, (src, peer) in enumerate(sources)
+    ]
+    for copy in halo_copies[:2]:
+        copy.start()
+
+    target = sector_ref[...].astype(F32)
+    block = block_ref[...].astype(F32)
+    offset = offset_ref[...].astype(F32)
+    resid = left_ref[...]
     sector_rows = -(-n // 16) * 16
     sector_iota = lax.broadcasted_iota(jnp.int32, (sector_rows, ray_count), 0).astype(F32)
     hits = (sector_iota == target).astype(F32)
@@ -105,7 +128,7 @@
     rank_all = dot(hits.astype(BF16), jnp.where(before, 1.0, 0.0).astype(BF16))
     slot = target * capp + jnp.sum(hits * rank_all, axis=0, keepdims=True)
 
-    offset_col = jnp.transpose(rows_ref[...])[:, 2:3].astype(jnp.int32)
+    offset_col = jnp.transpose(jnp.broadcast_to(offset, (8, ray_count)))[:, 0:1].astype(jnp.int32)
     turned = w_ref[...].astype(F32)
     for bit in range(7):
         on = lax.rem(offset_col // (1 << bit), 2) == 1
@@ -138,8 +161,6 @@
     lax.fori_loop(0, n, fill, 0)
     rays[g, me] = msg[me]
 
-    pl.semaphore_wait(barrier, n + 1)
-
     def route(d):
         peer = lax.rem(me + d, n)
         return pltpu.make_async_remote_copy(
@@ -184,22 +205,37 @@
 
         lax.fori_loop(0, share // TILE, outer, 0)
 
-    own = pl.ds(q0, share)
-    sources = [
-        (v_ref.at[1, own], right),
-        (v_ref.at[0, own], left),
-        (psend.at[1], right),
-        (psend.at[0], left),
-    ]
-    halo_copies = [
-        pltpu.make_async_remote_copy(
-            src, halo.at[i, own], h_send.at[i], h_recv.at[i],
-            device_id=(peer, g), device_id_type=MESH,
-        )
-        for i, (src, peer) in enumerate(sources)
-    ]
-    for copy in halo_copies:
+    for copy in halo_copies[2:]:
         copy.start()
+
+    def along_y(d):
+        src = rays.at[g, lax.rem(me - d + n, n)]
+        return pltpu.make_async_remote_copy(
+            src, src, y_send.at[d], y_recv.at[d], device_id=(me, gy), device_id_type=MESH
+        )
+
+    def along_c(d):
+        src = rays.at[g, lax.rem(me - d + n, n)]
+        return pltpu.make_async_remote_copy(
+            src, src, c_send.at[d], c_recv.at[d], device_id=(me, gc), device_id_type=MESH
+        )
+
+    def along_d(d):
+        src = rays.at[gy, lax.rem(me - d + n, n)]
+        return pltpu.make_async_remote_copy(
+            src, src, d_send.at[d], d_recv.at[d], device_id=(me, gc), device_id_type=MESH
+        )
+
+    along_y(0).start()
+    along_c(0).start()
+
+    def pass_on(d, carry):
+        route(d).wait_recv()
+        along_y(d).start()
+        along_c(d).start()
+        return carry
+
+    lax.fori_loop(1, n, pass_on, 0)
 
     def split(t, carry):
         rows = pl.ds(pl.multiple_of(t * TILE, TILE), TILE)
@@ -214,34 +250,19 @@
 
     lax.fori_loop(0, lat // TILE, split, 0)
 
-    def along_y(d):
-        src = rays.at[g, lax.rem(me - d + n, n)]
-        return pltpu.make_async_remote_copy(
-            src, src, y_send.at[d], y_recv.at[d], device_id=(me, gy), device_id_type=MESH
-        )
-
-    def along_c(d):
-        src = rays.at[g, lax.rem(me - d + n, n)]
-        return pltpu.make_async_remote_copy(
-            src, src, c_send.at[d], c_recv.at[d], device_id=(me, gc), device_id_type=MESH
-        )
-
-    def along_d(d):
-        src = rays.at[gy, lax.rem(me - d + n, n)]
-        return pltpu.make_async_remote_copy(
-            src, src, d_send.at[d], d_recv.at[d], device_id=(me, gc), device_id_type=MESH
-        )
-
-    along_y(0).start()
-    along_c(0).start()
-
-    def pass_on(d, carry):
-        route(d).wait_recv()
-        along_y(d).start()
-        along_c(d).start()
-        return carry
-
-    lax.fori_loop(1, n, pass_on, 0)
+    for layer in range(2):
+
+        def inner(t, carry, layer=layer):
+            start = pl.multiple_of(t * TILE, TILE)
+            rows = pl.ds(start, TILE)
+            plane, _ = planar(v_ref, layer, start)
+            sr_ref[layer, rows, :] = (
+                ratio * (plane - k0 * v_ref[1 - layer, rows, :])
+                - alpha * resid_ref[layer, rows, :]
+            )
+            return carry
+
+        lax.fori_loop(0, lat // TILE, inner, 0)
 
     def pass_again(d, carry):
         along_y(d).wait_recv()
@@ -250,25 +271,31 @@
 
     lax.fori_loop(0, n, pass_again, 0)
 
-    hy = []
-    hc = []
-    for i in range(4):
-        halo_copies[i].wait_recv()
-        piece = halo.at[i, own]
-        hy.append(
+    def piece_to(rows, sends, recvs, to):
+        return [
             pltpu.make_async_remote_copy(
-                piece, piece, hy_send.at[i], hy_recv.at[i],
-                device_id=(me, gy), device_id_type=MESH,
+                halo.at[i, rows], halo.at[i, rows], sends.at[i], recvs.at[i],
+                device_id=(me, to), device_id_type=MESH,
             )
-        )
-        hc.append(
-            pltpu.make_async_remote_copy(
-                piece, piece, hc_send.at[i], hc_recv.at[i],
-                device_id=(me, gc), device_id_type=MESH,
-            )
-        )
-        hy[i].start()
-        hc[i].start()
+            for i in range(4)
+        ]
+
+    hy = piece_to(own, hy_send, hy_recv, gy)
+    hc = piece_to(own, hc_send, hc_recv, gc)
+    hd = piece_to(pl.ds(qy0, share), hd_send, hd_recv, gc)
+
+    def halo_on(first):
+        for i in (first, first + 1):
+            halo_copies[i].wait_recv()
+            hy[i].start()
+            hc[i].start()
+
+    def halo_again(first):
+        for i in (first, first + 1):
+            hy[i].wait_recv()
+            hd[i].start()
+
+    halo_on(0)
 
     def settle(d, carry):
         along_c(d).wait_recv()
@@ -333,19 +360,12 @@
         return square + raw * raw
 
     chunks = groups * per_group
-    square = lax.fori_loop(0, chunks // 2, ray_chunk, jnp.zeros((1, chunk), F32))
-    hd = []
-    for i in range(4):
-        hy[i].wait_recv()
-        piece = halo.at[i, pl.ds(qy0, share)]
-        hd.append(
-            pltpu.make_async_remote_copy(
-                piece, piece, hd_send.at[i], hd_recv.at[i],
-                device_id=(me, gc), device_id_type=MESH,
-            )
-        )
-        hd[i].start()
-    square = lax.fori_loop(chunks // 2, chunks, ray_chunk, square)
+    square = jnp.zeros((1, chunk), F32)
+    bounds = [chunks * i // 8 for i in (0, 1, 4, 7, 8)]
+    for i, step in enumerate((lambda: halo_on(2), lambda: halo_again(0), lambda: halo_again(2), None)):
+        square = lax.fori_loop(bounds[i], bounds[i + 1], ray_chunk, square)
+        if step is not None:
+            step()
     ray_square = jnp.sum(square)
     for i in range(4):
         hc[i].wait_recv()
@@ -361,9 +381,7 @@
         def forward(t, total, layer=layer):
             start = pl.multiple_of(t * TILE, TILE)
             rows = pl.ds(start, TILE)
-            plane, _ = planar(v_ref, layer, start)
-            beside = halo[layer, rows, :] + v_ref[1 - layer, rows, :]
-            raw = ratio * (plane - k0 * beside) - alpha * resid_ref[layer, rows, :]
+            raw = sr_ref[layer, rows, :] - (ratio * k0) * halo[layer, rows, :]
             sr_ref[layer, rows, :] = raw
             return total + fold(raw * raw)
 
@@ -433,8 +451,39 @@
     total, home = lax.fori_loop(
         0, n, collect, (jnp.zeros((8, LANES), F32), jnp.zeros((8, ray_count), F32))
     )
-    sums_ref[...] = total
-    home_ref[...] = home
+
+    def number_of(i):
+        return jnp.broadcast_to(total[1:2, i : i + 1], (8, LANES))
+
+    rho_bar = scalar_ref[1]
+    phi_bar = scalar_ref[2]
+    beta = jnp.sqrt(number_of(0) / rows_total + EPSILON)
+    scale = 1.0 / (beta * ratio)
+    spread_sum = (
+        scale * scale * number_of(1)
+        - 2.0 * (scale * beta) * number_of(2)
+        + beta * beta * number_of(3)
+    )
+    alpha_new = jnp.sqrt(jnp.maximum(spread_sum, 0.0) / cells_total + EPSILON)
+    rho = jnp.sqrt(rho_bar * rho_bar + beta * beta)
+    cosine = rho_bar / rho
+    sine = beta / rho
+    results = [
+        alpha_new,
+        beta,
+        -cosine * alpha_new,
+        sine * phi_bar,
+        cosine * phi_bar / rho,
+        sine * alpha_new / rho,
+        scale / alpha_new,
+        beta / alpha_new,
+        1.0 / beta,
+    ]
+    tile = jnp.zeros((8, LANES), F32)
+    for i, result in enumerate(results):
+        tile = jnp.where(col == i, result, tile)
+    coef_ref[...] = tile
+    home_ref[...] = home / beta[:, 0:1]
 
     def finish(d, carry):
         route(d).wait_send()
@@ -452,6 +501,18 @@
     lax.fori_loop(0, n, finish_all, 0)
     for copy in halo_copies + hy + hc + hd:
         copy.wait_send()
+
+
+def update(coef, raw, back, v, search, model, model_new, search_new, dir_new, smooth_new):
+    def value(i):
+        return coef[0:1, i : i + 1]
+
+    for layer in range(2):
+        turned = back[layer] * value(6) - v[layer] * value(7)
+        dir_new[layer] = turned
+        search_new[layer] = turned - value(5) * search[layer]
+        model_new[layer] = model[layer] + value(4) * search[layer]
+        smooth_new[layer] = raw[layer] * value(8)
 
 
 def on_device(
@@ -478,25 +539,11 @@
     cells_total = lon_cells * lat * depth * n
     rows_total = ray_count * n * groups + cells_total
     ratio = math.sqrt(rows_total / cells_total)
-    rows = jnp.concatenate(
-        [
-            jnp.stack(
-                [
-                    ray_sector[:, 0].astype(F32),
-                    ray_block.astype(F32),
-                    ray_offset.astype(F32),
-                    ray_resid.astype(BF16).astype(F32),
-                ]
-            ),
-            jnp.zeros((4, ray_count), F32),
-        ]
-    )
-    coef = jnp.concatenate([stencil_coeffs, lsqr_scalars])
     field = jax.ShapeDtypeStruct((2, lat, depth), F32)
     vmem = pl.BlockSpec(memory_space=pltpu.VMEM)
     dma = pltpu.SemaphoreType.DMA
-    cfg = (n, groups, capp, ray_count, lat, depth, ratio)
-    smooth_raw, back, home, sums = pl.pallas_call(
+    cfg = (n, groups, capp, ray_count, lat, depth, ratio, rows_total, cells_total)
+    smooth_raw, back, home, coef = pl.pallas_call(
         functools.partial(kernel, cfg),
         out_shape=(
             field,
@@ -504,7 +551,7 @@
             jax.ShapeDtypeStruct((8, ray_count), F32),
             jax.ShapeDtypeStruct((8, LANES), F32),
         ),
-        in_specs=[pl.BlockSpec(memory_space=pltpu.SMEM)] + [vmem] * 4,
+        in_specs=[pl.BlockSpec(memory_space=pltpu.SMEM)] * 2 + [vmem] * 7,
         out_specs=(vmem,) * 4,
         scratch_shapes=[
             pltpu.VMEM((n, capp + META, LANES), BF16),
@@ -527,34 +574,33 @@
         cost_estimate=pl.CostEstimate(
             flops=20_000_000_000, bytes_accessed=8_000_000, transcendentals=0
         ),
-    )(coef, rows, ray_weights, model_dir, smooth_resid)
-
-    alpha_now = lsqr_scalars[0]
-    rho_bar = lsqr_scalars[1]
-    phi_bar = lsqr_scalars[2]
-    beta_now = jnp.sqrt(sums[1, 0] / rows_total + EPSILON)
-    scale = 1.0 / (beta_now * ratio)
-    alpha_total = (
-        scale * scale * sums[1, 1]
-        - 2.0 * (scale * beta_now) * sums[1, 2]
-        + beta_now * beta_now * sums[1, 3]
+    )(
+        stencil_coeffs,
+        lsqr_scalars,
+        ray_sector.reshape(1, ray_count),
+        ray_block.reshape(1, ray_count),
+        ray_offset.reshape(1, ray_count),
+        ray_resid.reshape(1, ray_count),
+        ray_weights,
+        model_dir,
+        smooth_resid,
     )
-    alpha_new = jnp.sqrt(jnp.maximum(alpha_total, 0.0) / cells_total + EPSILON)
-    rho_now = jnp.sqrt(rho_bar * rho_bar + beta_now * beta_now)
-    cosine = rho_bar / rho_now
-    sine = beta_now / rho_now
-    theta_now = sine * alpha_new
-    rho_bar_new = -cosine * alpha_new
-    phi_now = cosine * phi_bar
-    phi_bar_new = sine * phi_bar
-    beta_inverse = 1.0 / beta_now
-    dir_new = back * (scale / alpha_new) - model_dir * (beta_now / alpha_new)
-    smooth_new = smooth_raw * beta_inverse
-    ray_resid_new = home[0] * beta_inverse
-    model_new = model + phi_now / rho_now * search_dir
-    search_new = dir_new - theta_now / rho_now * search_dir
-    scalars_new = jnp.stack([alpha_new, beta_now, rho_bar_new, phi_bar_new])
-    return (model_new, search_new, dir_new, ray_resid_new, smooth_new, scalars_new)
+
+    lat_block = math.gcd(lat, 64)
+    whole = pl.BlockSpec((8, LANES), lambda t: (0, 0))
+    part = pl.BlockSpec((2, lat_block, depth), lambda t: (0, t, 0))
+    model_new, search_new, dir_new, smooth_new = pl.pallas_call(
+        update,
+        grid=(lat // lat_block,),
+        out_shape=(field,) * 4,
+        in_specs=[whole] + [part] * 5,
+        out_specs=(part,) * 4,
+        compiler_params=pltpu.CompilerParams(vmem_limit_bytes=24 * 1024 * 1024),
+        cost_estimate=pl.CostEstimate(
+            flops=10_000_000, bytes_accessed=18_874_368, transcendentals=0
+        ),
+    )(coef, smooth_raw, back, model_dir, search_dir, model)
+    return (model_new, search_new, dir_new, home[0], smooth_new, coef[0, :4])
 
 
 def solution(mesh):

time: 114 us -> 95.7 us (0.84)
  other arithmetic: 12.2 us -> 0 us
  between operations: 6.67 us -> 0.66 us
  local copies, waits for them, and re-layouts: 4.15 us -> 6.03 us
  Pallas kernels: 90.5 us -> 88.8 us
    sub x1 -> x0, other arithmetic: 7.59 us -> none  [on_device(): search_new = dir_new - theta_now / rho_now * search_dir]
    pallas_call x1, Pallas kernels: 90.5 us -> 83.2 us  [on_device(): pl.pallas_call(functools.partial(kernel, cfg), out_shape=(field, field, j...]
    pallas_call x0 -> x1, Pallas kernels: none -> 5.59 us  [on_device(): pl.pallas_call(update, grid=(lat // lat_block,), out_shape=(field,) * 4,...]
    unnamed x4 -> x20, local copies, waits for them, and re-layouts: 2.21 us -> 4.94 us
    convert_element_type x3 -> x0, other arithmetic: 2.05 us -> none  [the longest x1 0.69 us: on_device(): ray_sector[:, 0].astype(F32)]
    slice x2 -> x1, local copies, waits for them, and re-layouts: 1.9 us -> 0.58 us  [on_device(): return (model_new, search_new, dir_new, home[0], smooth_new, coef[0, :4])]
    another operation x2 -> x0, other arithmetic: 1.27 us -> none  [the longest x1 0.68 us: on_device(): jnp.stack([ray_sector[:, 0].astype(F32), ray_block.astype(F32), ray_offse...]
where the time goes in v2:
time: 95.7 us; the launch traced here: 95.5 us
  Pallas kernels  88.8 us (93%)
  local copies, waits for them, and re-layouts  6.03 us (6%)
    pallas_call x1, Pallas kernels, on_device(): pl.pallas_call(functools.partial(kernel, cfg), out_shape=(field, field, j...  83.2 us
    pallas_call x1, Pallas kernels, on_device(): pl.pallas_call(update, grid=(lat // lat_block,), out_shape=(field,) * 4,...  5.59 us
    unnamed x20, local copies, waits for them, and re-layouts  4.94 us

profile of v2, /device:TPU:0, one launch (start us, length us, event | category | flops | bytes accessed | tf_op | source)
XLA Modules:
  0.0 95.5 jit_solution(9243969737499937467)
XLA Ops:
  0.6 0.0 copy-start.3
  0.6 0.9 copy-done.3
  1.5 0.0 copy-start.4
  1.5 0.7 copy-done.4
  2.2 0.0 copy-start.5
  2.2 0.7 copy-done.5
  2.9 0.0 copy-start.6
  2.9 0.7 copy-done.6
  3.6 0.0 copy-start.7
  3.6 0.7 copy-done.7
  4.3 0.0 copy-start.8
  4.3 0.7 copy-done.8
  4.9 0.0 copy-start.9
  4.9 0.7 copy-done.9
  5.6 0.0 copy-start
  5.6 0.0 copy-start.1
  5.6 0.0 copy-start.2
  5.6 83.2 %shard_map.154 = (f32[2,512,512]{2,1,0:T(8,128)S(1)}, f32[2,512,512]{2,1,0:T(8,128)S(1)}, f32[8,512]{1,0:T(8,128)S(1)}, f32[8,128]{1,0:T(8,128)S(1)}) custom-call(f32[4]{0:T(128)S(1)} %copy-done.8, f32[3]{0:T(128)S(1)} %copy-done.9, s32[1,512]{1,0:T(1,128)S(1)} %bitcast.7, s32[1,512]{1,0:T(1,128)S(1)} %bitcast.8, s32[1,512]{1,0:T(1,128)S(1)} %bitcast.9, ...), custom_call_target="tpu_custom_call" | custom-call | flops 20000000000 | bytes 8000000 | tf_op jit(solution)/shard_map/pallas_call | solution.py:546
  88.8 0.5 slice_bitcast_fusion
  89.3 0.6 slice.6
  89.9 0.0 copy-done
  89.9 0.0 copy-done.1
  89.9 0.0 copy-done.2
  89.9 5.6 %shard_map.155 = (f32[2,512,512]{2,1,0:T(8,128)}, f32[2,512,512]{2,1,0:T(8,128)}, f32[2,512,512]{2,1,0:T(8,128)}, f32[2,512,512]{2,1,0:T(8,128)}) custom-call(f32[8,128]{1,0:T(8,128)S(1)} %get-tuple-element.14.coef, f32[2,512,512]{2,1,0:T(8,128)S(1)} %get-tuple-element.15.raw, f32[2,512,512]{2,1,0:T(8,128)S(1)} %get-tuple-element.16.back, ...), custom_call_target="tpu_custom_call" | custom-call | flops 10000000 | bytes 18874368 | tf_op jit(solution)/shard_map/pallas_call | solution.py:592
Async XLA Ops:
  0.6 0.9 copy-start.3
  1.5 0.7 copy-start.4
  2.2 0.7 copy-start.5
  2.9 0.7 copy-start.6
  3.6 0.7 copy-start.7
  4.3 0.7 copy-start.8
  4.9 0.7 copy-start.9
  5.6 84.3 %copy-start = (f32[2,512,512]{2,1,0:T(8,128)S(1)}, f32[2,512,512]{2,1,0:T(8,128)}, u32[]{:S(2)}) copy-start(f32[2,512,512]{2,1,0:T(8,128)} %v.1) | copy-start | bytes 6291460
  5.6 84.3 %copy-start.1 = (f32[2,512,512]{2,1,0:T(8,128)S(1)}, f32[2,512,512]{2,1,0:T(8,128)}, u32[]{:S(2)}) copy-start(f32[2,512,512]{2,1,0:T(8,128)} %search.1) | copy-start | bytes 6291460
  5.6 84.3 %copy-start.2 = (f32[2,512,512]{2,1,0:T(8,128)S(1)}, f32[2,512,512]{2,1,0:T(8,128)}, u32[]{:S(2)}) copy-start(f32[2,512,512]{2,1,0:T(8,128)} %model.1) | copy-start | bytes 6291460

commit v3 on v2

--- a/solution.py
+++ b/solution.py
@@ -28,10 +28,10 @@
     cfg,
     stencil_ref,
     scalar_ref,
-    sector_ref,
-    block_ref,
-    offset_ref,
-    left_ref,
+    sector_hbm,
+    block_hbm,
+    offset_hbm,
+    left_hbm,
     w_ref,
     v_ref,
     resid_ref,
@@ -67,6 +67,11 @@
     hd_recv,
     r_send,
     r_recv,
+    sector_ref,
+    block_ref,
+    offset_ref,
+    left_ref,
+    l_sem,
 ):
     n, groups, capp, ray_count, lat, depth, ratio, rows_total, cells_total = cfg
     me = lax.axis_index("lon")
@@ -84,6 +89,20 @@
     diag = 2.0 * (k0 + k1 + k2) + stencil_ref[3]
     alpha = scalar_ref[0]
 
+    loads = [
+        pltpu.make_async_copy(src, dst, l_sem.at[i])
+        for i, (src, dst) in enumerate(
+            (
+                (sector_hbm, sector_ref),
+                (block_hbm, block_ref),
+                (offset_hbm, offset_ref),
+                (left_hbm, left_ref),
+            )
+        )
+    ]
+    for load in loads:
+        load.start()
+
     barrier = pltpu.get_barrier_semaphore()
 
     def greet(d, carry):
@@ -114,6 +133,9 @@
     ]
     for copy in halo_copies[:2]:
         copy.start()
+
+    for load in loads:
+        load.wait()
 
     target = sector_ref[...].astype(F32)
     block = block_ref[...].astype(F32)
@@ -551,7 +573,7 @@
             jax.ShapeDtypeStruct((8, ray_count), F32),
             jax.ShapeDtypeStruct((8, LANES), F32),
         ),
-        in_specs=[pl.BlockSpec(memory_space=pltpu.SMEM)] * 2 + [vmem] * 7,
+        in_specs=[pl.BlockSpec(memory_space=pltpu.SMEM)] * 2 + [pl.BlockSpec(memory_space=pl.ANY)] * 4 + [vmem] * 3,
         out_specs=(vmem,) * 4,
         scratch_shapes=[
             pltpu.VMEM((n, capp + META, LANES), BF16),
@@ -567,7 +589,9 @@
         ]
         + [dma((n,))] * 8
         + [dma((4,))] * 8
-        + [dma((n,))] * 2,
+        + [dma((n,))] * 2
+        + [pltpu.VMEM((1, ray_count), jnp.int32)] * 3
+        + [pltpu.VMEM((1, ray_count), F32), dma((4,))],
         compiler_params=pltpu.CompilerParams(
             collective_id=0, has_side_effects=True, vmem_limit_bytes=48 * 1024 * 1024
         ),

time: 95.7 us -> 95.7 us (level)
  no operation moved by 1% of the time
where the time goes in v3:
time: 95.7 us; the launch traced here: 95.4 us
  Pallas kernels  88.7 us (93%)
  local copies, waits for them, and re-layouts  6.03 us (6%)
    pallas_call x1, Pallas kernels, on_device(): pl.pallas_call(functools.partial(kernel, cfg), out_shape=(field, field, j...  83.1 us
    pallas_call x1, Pallas kernels, on_device(): pl.pallas_call(update, grid=(lat // lat_block,), out_shape=(field,) * 4,...  5.59 us
    unnamed x20, local copies, waits for them, and re-layouts  4.94 us

profile of v3, /device:TPU:0, one launch (start us, length us, event | category | flops | bytes accessed | tf_op | source)
XLA Modules:
  0.0 95.4 jit_solution(1193734389944990336)
XLA Ops:
  0.6 0.0 copy-start.3
  0.6 0.9 copy-done.3
  1.5 0.0 copy-start.4
  1.5 0.7 copy-done.4
  2.2 0.0 copy-start.5
  2.2 0.7 copy-done.5
  2.9 0.0 copy-start.6
  2.9 0.7 copy-done.6
  3.6 0.0 copy-start.7
  3.6 0.7 copy-done.7
  4.3 0.0 copy-start.8
  4.3 0.7 copy-done.8
  4.9 0.0 copy-start.9
  4.9 0.7 copy-done.9
  5.6 0.0 copy-start
  5.6 0.0 copy-start.1
  5.6 0.0 copy-start.2
  5.6 83.1 %shard_map.154 = (f32[2,512,512]{2,1,0:T(8,128)S(1)}, f32[2,512,512]{2,1,0:T(8,128)S(1)}, f32[8,512]{1,0:T(8,128)S(1)}, f32[8,128]{1,0:T(8,128)S(1)}) custom-call(f32[4]{0:T(128)S(1)} %copy-done.8, f32[3]{0:T(128)S(1)} %copy-done.9, s32[1,512]{1,0:T(1,128)S(1)} %bitcast.7, s32[1,512]{1,0:T(1,128)S(1)} %bitcast.8, s32[1,512]{1,0:T(1,128)S(1)} %bitcast.9, ...), custom_call_target="tpu_custom_call" | custom-call | flops 20000000000 | bytes 8000000 | tf_op jit(solution)/shard_map/pallas_call | solution.py:568
  88.7 0.5 slice_bitcast_fusion
  89.2 0.6 slice.6
  89.8 0.0 copy-done
  89.8 0.0 copy-done.1
  89.8 0.0 copy-done.2
  89.8 5.6 %shard_map.155 = (f32[2,512,512]{2,1,0:T(8,128)}, f32[2,512,512]{2,1,0:T(8,128)}, f32[2,512,512]{2,1,0:T(8,128)}, f32[2,512,512]{2,1,0:T(8,128)}) custom-call(f32[8,128]{1,0:T(8,128)S(1)} %get-tuple-element.14.coef, f32[2,512,512]{2,1,0:T(8,128)S(1)} %get-tuple-element.15.raw, f32[2,512,512]{2,1,0:T(8,128)S(1)} %get-tuple-element.16.back, ...), custom_call_target="tpu_custom_call" | custom-call | flops 10000000 | bytes 18874368 | tf_op jit(solution)/shard_map/pallas_call | solution.py:616
Async XLA Ops:
  0.6 0.9 copy-start.3
  1.5 0.7 copy-start.4
  2.2 0.7 copy-start.5
  2.9 0.7 copy-start.6
  3.6 0.7 copy-start.7
  4.3 0.7 copy-start.8
  4.9 0.7 copy-start.9
  5.6 84.2 %copy-start = (f32[2,512,512]{2,1,0:T(8,128)S(1)}, f32[2,512,512]{2,1,0:T(8,128)}, u32[]{:S(2)}) copy-start(f32[2,512,512]{2,1,0:T(8,128)} %v.1) | copy-start | bytes 6291460
  5.6 84.2 %copy-start.1 = (f32[2,512,512]{2,1,0:T(8,128)S(1)}, f32[2,512,512]{2,1,0:T(8,128)}, u32[]{:S(2)}) copy-start(f32[2,512,512]{2,1,0:T(8,128)} %search.1) | copy-start | bytes 6291460
  5.6 84.2 %copy-start.2 = (f32[2,512,512]{2,1,0:T(8,128)S(1)}, f32[2,512,512]{2,1,0:T(8,128)}, u32[]{:S(2)}) copy-start(f32[2,512,512]{2,1,0:T(8,128)} %model.1) | copy-start | bytes 6291460
